TPU v7x, 32 devices: a whole 2x2x4 slice. The times are simulated.
32 devices in a mesh: section: 1, expert: 32 (over z, y, x, core).
Axes of the slice: x: 2, y: 2, z: 4, core: 2. Of those that a mesh axis runs over, the one named last changes fastest.
Arguments:
- feat_saved: bfloat16 [1, 2, 4096, 1024], P('section', None, 'expert'), may hold values from -6 to 6
- out_grad: bfloat16 [2, 4096, 1024], P(None, 'expert'), may hold values from -6 to 6
- lengths: int32 [2, 32], P(None, 'expert'), may hold values from 32 to 128, as said below
- expert_ids: int32 [1, 2, 4096], P('section', None, 'expert'), may hold values from 0 to 31, as said below
- slot_ids: int32 [1, 2, 4096], P('section', None, 'expert'), may hold values from 0 to 5, as said below
- expert_preact: bfloat16 [1, 2, 6144, 640], P('section', None, 'expert'), may hold values from -6 to 6
- conv_weight: bfloat16 [1, 32, 1024], P('section'), may hold values from -0.5 to 0.5
- norm_gain: bfloat16 [1, 1024], P('section'), may hold values from 0.5 to 1.5
- centroids: bfloat16 [1, 32, 1024], P('section'), may hold values from -0.375 to 0.375
- w_in: bfloat16 [1, 32, 1024, 640], P('section', 'expert'), may hold values from -0.1875 to 0.1875
- w_out: bfloat16 [1, 32, 640, 1024], P('section', 'expert'), may hold values from -0.25 to 0.25
Outputs:
- section_grads: bfloat16 [1, 2, 4096, 1024], P('section', None, 'expert')
Inputs may be any that keep to these rules, and one draw needn't show every extreme that they name: `expert_ids`: in every block and micro-batch, the 128 frames of one utterance name each expert at most 6 times, and one expert is named exactly 6 times by the frames of every utterance. `slot_ids`: within one utterance's frames of one block and micro-batch, the frames that name the same expert hold the slots 0, 1, ... up to their count less one, each once. `lengths`: in every micro-batch at least one utterance has all 128 frames.
All inputs are finite; a program needn't handle non-finite values.
Results may differ from a plain program's by a relative error of at most 0.02.
Values may be sent and summed in bfloat16 or wider, within the bound.
A program may use at most 64 MiB of HBM per device.

v0:
```python
import math

import jax
import jax.numpy as jnp
from jax import lax
from jax.sharding import PartitionSpec as P


def shifted(block, axis, distance):
    devices = range(lax.axis_size(axis))
    route = [(i - distance, i) for i in devices if i - distance in devices]
    return lax.ppermute(block, axis, route)


def time_conv(values, kernel, low_pad):
    tap_count = kernel.shape[0]
    frames = values.shape[-2]
    widths = [(0, 0)] * (values.ndim - 2) + [(low_pad, tap_count - 1 - low_pad), (0, 0)]
    padded = jnp.pad(values, widths)
    summed = jnp.zeros_like(values)
    for tap_idx in range(tap_count):
        summed = summed + kernel[tap_idx] * lax.slice_in_dim(
            padded, tap_idx, tap_idx + frames, axis=values.ndim - 2
        )
    return summed


def gelu_parts(preact):
    act_val = preact.astype(jnp.float32)
    cdf_val = 0.5 * (1.0 + jax.scipy.special.erf(act_val * (1.0 / math.sqrt(2.0))))
    gelu_val = act_val * cdf_val
    gelu_slope = cdf_val + act_val * jnp.exp(-0.5 * act_val * act_val) * (
        1.0 / math.sqrt(2.0 * math.pi)
    )
    return (gelu_val, gelu_slope)


def contract_last(left, right):
    return lax.dot_general(
        left, right, (((1,), (1,)), ((), ())), preferred_element_type=jnp.float32
    )


def expert_whole(bucket, preact, weight_in, weight_out):
    received = lax.all_to_all(bucket, "expert", split_axis=0, concat_axis=0, tiled=True)
    recv_shape = received.shape
    slot_rows = received.reshape(recv_shape[0] * recv_shape[1], recv_shape[2])
    hidden_grad = contract_last(slot_rows, weight_out)
    gelu_val, gelu_slope = gelu_parts(preact)
    gate_grad = jnp.sum(hidden_grad * gelu_val, axis=1)
    pre_grad = (hidden_grad * gelu_slope).astype(jnp.bfloat16)
    slot_grad = contract_last(pre_grad, weight_in).astype(jnp.bfloat16)
    back_rows, back_gate = (
        lax.all_to_all(
            slot_grad.reshape(recv_shape), "expert", split_axis=0, concat_axis=0, tiled=True
        ),
        lax.all_to_all(
            gate_grad.reshape(recv_shape[0], recv_shape[1]).astype(jnp.bfloat16),
            "expert",
            split_axis=0,
            concat_axis=0,
            tiled=True,
        ).astype(jnp.float32),
    )
    return (back_rows.reshape(slot_rows.shape), back_gate.reshape(slot_rows.shape[0]))


def block_grad(
    grad_in,
    feats_b,
    length,
    routed,
    slot_pos,
    preact,
    conv_k,
    gain_vec,
    cent_table,
    weight_in,
    weight_out,
):
    frames, feat_width = feats_b.shape
    experts = cent_table.shape[0]
    slot_cap = preact.shape[0] // experts
    tap_count = conv_k.shape[0]
    feats = feats_b.astype(jnp.float32)
    frame_mask = (lax.iota(jnp.int32, frames) < length).astype(jnp.float32)[:, None]
    pre_act = time_conv(feats * frame_mask, conv_k, tap_count // 2)
    sig_pre = jax.nn.sigmoid(pre_act)
    residual = feats + frame_mask * pre_act * sig_pre
    inv_rms = lax.rsqrt(jnp.mean(residual * residual, axis=1, keepdims=True) + 1e-06)
    normed = (residual * inv_rms * gain_vec).astype(jnp.bfloat16)
    onehot_exp = (routed[:, None] == lax.iota(jnp.int32, experts)[None, :]).astype(jnp.bfloat16)
    score_all = jnp.dot(normed, cent_table.T, preferred_element_type=jnp.float32)
    score_val = jnp.sum(score_all * onehot_exp.astype(jnp.float32), axis=1)
    gate_val = jax.nn.sigmoid(score_val)
    cent_rows = jnp.dot(onehot_exp, cent_table, preferred_element_type=jnp.float32)
    grad_f = grad_in.astype(jnp.float32)
    conv_slope = frame_mask * sig_pre * (1.0 + pre_act * (1.0 - sig_pre))
    kernel_rev = conv_k[::-1]
    back_pad = tap_count - 1 - tap_count // 2
    target = routed * slot_cap + slot_pos
    onehot_slot = (lax.iota(jnp.int32, experts * slot_cap)[:, None] == target[None, :]).astype(
        jnp.bfloat16
    )
    bucket = jnp.dot(onehot_slot, grad_in, preferred_element_type=jnp.float32).astype(jnp.bfloat16)
    bucket = bucket.reshape(experts, slot_cap, feat_width)
    slot_back, gate_back = expert_whole(bucket, preact, weight_in, weight_out)
    slot_grad = lax.dot_general(
        onehot_slot, slot_back, (((0,), (0,)), ((), ())), preferred_element_type=jnp.float32
    )
    gate_grad = jnp.dot(gate_back, onehot_slot.astype(jnp.float32), precision=lax.Precision.HIGHEST)
    total_grad = (
        gate_val[:, None] * slot_grad
        + (gate_val * (1.0 - gate_val) * gate_grad)[:, None] * cent_rows
    )
    scaled = total_grad * gain_vec
    cubed = inv_rms * inv_rms * inv_rms
    norm_grad = inv_rms * scaled - residual * cubed * jnp.mean(
        residual * scaled, axis=1, keepdims=True
    )
    resid_grad = grad_f + norm_grad
    result = resid_grad + frame_mask * time_conv(conv_slope * resid_grad, kernel_rev, back_pad)
    return result.astype(jnp.bfloat16)


def on_device(
    feat_saved,
    out_grad,
    lengths,
    expert_ids,
    slot_ids,
    expert_preact,
    conv_weight,
    norm_gain,
    centroids,
    w_in,
    w_out,
):
    section_count = lax.axis_size("section")
    section_idx = lax.axis_index("section")
    micro_count = out_grad.shape[0]
    conv_k = conv_weight[0].astype(jnp.float32)
    gain_vec = norm_gain[0].astype(jnp.float32)
    cent_table = centroids[0]
    weight_in = w_in[0, 0]
    weight_out = w_out[0, 0]

    def one_tick(tick_idx, carry):
        incoming, grads = carry
        micro_pos = tick_idx - (section_count - 1 - section_idx)
        is_valid = jnp.logical_and(micro_pos >= 0, micro_pos < micro_count)
        micro_sel = jnp.clip(micro_pos, 0, micro_count - 1)

        def select_micro(array):
            return lax.dynamic_index_in_dim(array, micro_sel, 0, keepdims=False)

        grad_in = jnp.where(section_idx == section_count - 1, select_micro(out_grad), incoming)
        new_grad = block_grad(
            grad_in,
            select_micro(feat_saved[0]),
            select_micro(lengths)[0],
            select_micro(expert_ids[0]),
            select_micro(slot_ids[0]),
            select_micro(expert_preact[0]),
            conv_k,
            gain_vec,
            cent_table,
            weight_in,
            weight_out,
        )
        updated = lax.dynamic_update_index_in_dim(grads, new_grad, micro_sel, 0)
        grads = jnp.where(is_valid, updated, grads)
        incoming = shifted(new_grad, "section", -1)
        return (incoming, grads)

    start = (jnp.zeros(out_grad.shape[1:], jnp.bfloat16), jnp.zeros_like(out_grad))
    final_in, grads = lax.fori_loop(0, section_count + micro_count - 1, one_tick, start)
    return grads[None]


def solution(mesh):
    in_specs = (
        P("section", None, "expert", None),
        P(None, "expert", None),
        P(None, "expert"),
        P("section", None, "expert"),
        P("section", None, "expert"),
        P("section", None, "expert", None),
        P("section", None, None),
        P("section", None),
        P("section", None, None),
        P("section", "expert", None, None),
        P("section", "expert", None, None),
    )
    out_specs = P("section", None, "expert", None)
    return jax.shard_map(
        on_device, mesh=mesh, in_specs=in_specs, out_specs=out_specs, check_vma=False
    )
```

profile of v0, /device:TPU:0, one launch (start us, length us, event | category | flops | bytes accessed | tf_op | source)
XLA Modules:
  0.0 120.1 jit_solution(10963601440538976268)
XLA Ops:
  0.7 0.8 bitcast_convert_fusion
  1.6 117.7 %while.17 = (s32[]{:T(128)}, bf16[2,128,1024]{2,1,0:T(8,128)(2,1)S(1)}, bf16[2,128,1024]{2,1,0:T(8,128)(2,1)}, bf16[1,2,128,1024]{3,2,1,0:T(8,128)(2,1)}, s32[2,...) while((s32[]{:T(128)}, ...), condition=%wide.region_5.6_spmd, body=%wide.region_0.5_spmd.sunk | while | flops 645924160 | bytes 29062524 | solution.py:177
  2.3 1.3 %convolution_convert_fusion.4 = bf16[192,1024]{1,0:T(8,128)(2,1)S(1)} fusion(bf16[2,128,1024]{2,1,0:T(8,128)(2,1)} %get-tuple-element.658, s32[]{:T(128)S(6)} %min.13, s32[128]{0:T(128)S(1)} %get-tuple-element.615), kind=kOutput, calls=%fused_computation.63.clone.1 | convolution fusion | flops 50552832 | bytes 655876 | tf_op jit(solution)/shard_map/while/body/eval_jaxpr/dot_general | solution.py:105
  3.6 0.9 reshape.168
  4.5 7.3 %all-to-all-start = ((bf16[32,6,1024]{2,1,0:T(8,128)(2,1)}), bf16[32,6,1024]{2,1,0:T(8,128)(2,1)S(1)}, u32[]{:S(2)}, u32[]{:S(2)}) async-start(bf16[32,6,1024]{2,1,0:T(8,128)(2,1)} %reshape.168), calls=%async_computation | async-start | bytes 1048576 | tf_op jit(solution)/shard_map/while/body/eval_jaxpr/all_to_all | solution.py:45
  13.3 4.0 %multiply_reduce_fusion.4 = (f32[128]{0:T(128)S(1)}, f32[128,1024]{1,0:T(8,128)S(1)}, f32[128,1024]{1,0:T(8,128)S(1)}) fusion(f32[128]{0:T(128)S(1)} %compare_convert_fusion.2, bf16[1,2,128,1024]{3,2,1,0:T(8,128)(2,1)S(1)} %copy-done.1, s32[]{:T(128)S(6)} %min.13, f32[1024]{0:T(1024)S(1)} %bitcast.189, f32[1024]{0:T(1024)S(1)} %bitcast.191, ...), kind=kLoop, calls=%fused_computation.209.clone.1 | loop fusion | flops 9437056 | bytes 1967108 | tf_op jit(solution)/shard_map/while/body/eval_jaxpr/reduce_sum | solution.py:90
  17.3 10.1 %all-to-all-done = bf16[32,6,1024]{2,1,0:T(8,128)(2,1)S(1)} async-done(((bf16[32,6,1024]{2,1,0:T(8,128)(2,1)}), bf16[32,6,1024]{2,1,0:T(8,128)(2,1)S(1)}, u32[]{:S(2)}, u32[]{:S(2)}) %all-to-all-start) | async-done | bytes 393248 | tf_op jit(solution)/shard_map/while/body/eval_jaxpr/all_to_all | solution.py:45
  27.5 2.0 %fusion.203 = (bf16[192]{0:T(256)(128)(2,1)S(1)}, f32[192,640]{1,0:T(8,128)S(1)}) fusion(bf16[1,2,192,640]{3,2,1,0:T(8,128)(2,1)S(1)} %copy-done.4, s32[]{:T(128)S(6)} %min.13, bf16[192,1024]{1,0:T(8,128)(2,1)S(1)} %reshape.169, bf16[640,1024]{1,0:T(8,128)(2,1)} %get-tuple-element.666), kind=kOutput, calls=%fused_computation.221.clone.1 | convolution fusion | flops 252518208 | bytes 2441604 | tf_op jit(solution)/shard_map/while/body/eval_jaxpr/dot_general | solution.py:39
  29.6 0.7 convert_element_type.234
  30.3 3.1 %all-to-all-start.2 = ((bf16[32,1,6]{2,1,0:T(2,128)(2,1)}), bf16[32,1,6]{2,1,0:T(2,128)(2,1)S(1)}, u32[]{:S(2)}, u32[]{:S(2)}) async-start(bf16[32,1,6]{2,1,0:T(2,128)(2,1)} %convert_element_type.234), calls=%async_computation.2 | async-start | bytes 32768 | tf_op jit(solution)/shard_map/while/body/eval_jaxpr/all_to_all | solution.py:57
  33.4 2.0 %convolution_convert_fusion.5 = bf16[192,1024]{1,0:T(8,128)(2,1)S(1)} fusion(bf16[1024,640]{1,0:T(8,128)(2,1)} %get-tuple-element.668, f32[192,640]{1,0:T(8,128)S(1)} %get-tuple-element.616, bf16[1,2,192,640]{3,2,1,0:T(8,128)(2,1)S(1)} %copy-done.4, s32[]{:T(128)S(6)} %min.13), kind=kOutput, calls=%fused_computation.62.clone.1 | convolution fusion | flops 253206528 | bytes 2441220 | tf_op jit(solution)/shard_map/while/body/eval_jaxpr/dot_general | solution.py:39
  35.4 0.9 reshape.170
  36.3 4.2 %all-to-all-done.2 = bf16[32,1,6]{2,1,0:T(2,128)(2,1)S(1)} async-done(((bf16[32,1,6]{2,1,0:T(2,128)(2,1)}), bf16[32,1,6]{2,1,0:T(2,128)(2,1)S(1)}, u32[]{:S(2)}, u32[]{:S(2)}) %all-to-all-start.2) | async-done | bytes 416 | tf_op jit(solution)/shard_map/while/body/eval_jaxpr/all_to_all | solution.py:57
  40.5 2.6 %all-to-all-start.1 = ((bf16[32,6,1024]{2,1,0:T(8,128)(2,1)}), bf16[32,6,1024]{2,1,0:T(8,128)(2,1)S(1)}, u32[]{:S(2)}, u32[]{:S(2)}) async-start(bf16[32,6,1024]{2,1,0:T(8,128)(2,1)} %reshape.170), calls=%async_computation.1 | async-start | bytes 1048576 | tf_op jit(solution)/shard_map/while/body/eval_jaxpr/all_to_all | solution.py:54
  43.8 14.9 %all-to-all-done.1 = bf16[32,6,1024]{2,1,0:T(8,128)(2,1)S(1)} async-done(((bf16[32,6,1024]{2,1,0:T(8,128)(2,1)}), bf16[32,6,1024]{2,1,0:T(8,128)(2,1)S(1)}, u32[]{:S(2)}, u32[]{:S(2)}) %all-to-all-start.1) | async-done | bytes 393248 | tf_op jit(solution)/shard_map/while/body/eval_jaxpr/all_to_all | solution.py:54
  60.2 2.4 %fusion.206 = bf16[2,128,1024]{2,1,0:T(8,128)(2,1)S(1)} fusion(bf16[2,128,1024]{2,1,0:T(8,128)(2,1)S(1)} %get-tuple-element.641, s32[]{:T(128)S(6)} %min.13, pred[]{:T(512)S(6)} %ge.12, f32[128,1024]{1,0:T(8,128)S(1)} %multiply_multiply_fusion.5, f32[1024]{0:T(1024)S(1)} %bitcast.188, f32[1024]{0:T(1024)S(1)} %bitcast.226, f32[1024]{0:T(1024)S(1)} %bitcast.250, ...), kind=kLoop, calls=%fused_computation.223.clone.1 | loop fusion | flops 9568256 | bytes 2492421 | tf_op jit(solution)/shard_map/while/body/eval_jaxpr/jit(_where)/select_n | solution.py:172
  62.6 0.7 fusion.202
  63.3 1.3 %convolution_convert_fusion.4 = bf16[192,1024]{1,0:T(8,128)(2,1)S(1)} fusion(bf16[2,128,1024]{2,1,0:T(8,128)(2,1)} %get-tuple-element.658, s32[]{:T(128)S(6)} %min.13, s32[128]{0:T(128)S(1)} %get-tuple-element.615), kind=kOutput, calls=%fused_computation.63.clone.1 | convolution fusion | flops 50552832 | bytes 655876 | tf_op jit(solution)/shard_map/while/body/eval_jaxpr/dot_general | solution.py:105
  64.6 0.9 reshape.168
  65.5 3.0 %all-to-all-start = ((bf16[32,6,1024]{2,1,0:T(8,128)(2,1)}), bf16[32,6,1024]{2,1,0:T(8,128)(2,1)S(1)}, u32[]{:S(2)}, u32[]{:S(2)}) async-start(bf16[32,6,1024]{2,1,0:T(8,128)(2,1)} %reshape.168), calls=%async_computation | async-start | bytes 1048576 | tf_op jit(solution)/shard_map/while/body/eval_jaxpr/all_to_all | solution.py:45
  69.9 4.0 %multiply_reduce_fusion.4 = (f32[128]{0:T(128)S(1)}, f32[128,1024]{1,0:T(8,128)S(1)}, f32[128,1024]{1,0:T(8,128)S(1)}) fusion(f32[128]{0:T(128)S(1)} %compare_convert_fusion.2, bf16[1,2,128,1024]{3,2,1,0:T(8,128)(2,1)S(1)} %copy-done.1, s32[]{:T(128)S(6)} %min.13, f32[1024]{0:T(1024)S(1)} %bitcast.189, f32[1024]{0:T(1024)S(1)} %bitcast.191, ...), kind=kLoop, calls=%fused_computation.209.clone.1 | loop fusion | flops 9437056 | bytes 1967108 | tf_op jit(solution)/shard_map/while/body/eval_jaxpr/reduce_sum | solution.py:90
  73.9 10.1 %all-to-all-done = bf16[32,6,1024]{2,1,0:T(8,128)(2,1)S(1)} async-done(((bf16[32,6,1024]{2,1,0:T(8,128)(2,1)}), bf16[32,6,1024]{2,1,0:T(8,128)(2,1)S(1)}, u32[]{:S(2)}, u32[]{:S(2)}) %all-to-all-start) | async-done | bytes 393248 | tf_op jit(solution)/shard_map/while/body/eval_jaxpr/all_to_all | solution.py:45
  84.2 2.0 %fusion.203 = (bf16[192]{0:T(256)(128)(2,1)S(1)}, f32[192,640]{1,0:T(8,128)S(1)}) fusion(bf16[1,2,192,640]{3,2,1,0:T(8,128)(2,1)S(1)} %copy-done.4, s32[]{:T(128)S(6)} %min.13, bf16[192,1024]{1,0:T(8,128)(2,1)S(1)} %reshape.169, bf16[640,1024]{1,0:T(8,128)(2,1)} %get-tuple-element.666), kind=kOutput, calls=%fused_computation.221.clone.1 | convolution fusion | flops 252518208 | bytes 2441604 | tf_op jit(solution)/shard_map/while/body/eval_jaxpr/dot_general | solution.py:39
  86.2 0.7 convert_element_type.234
  87.0 3.1 %all-to-all-start.2 = ((bf16[32,1,6]{2,1,0:T(2,128)(2,1)}), bf16[32,1,6]{2,1,0:T(2,128)(2,1)S(1)}, u32[]{:S(2)}, u32[]{:S(2)}) async-start(bf16[32,1,6]{2,1,0:T(2,128)(2,1)} %convert_element_type.234), calls=%async_computation.2 | async-start | bytes 32768 | tf_op jit(solution)/shard_map/while/body/eval_jaxpr/all_to_all | solution.py:57
  90.1 2.0 %convolution_convert_fusion.5 = bf16[192,1024]{1,0:T(8,128)(2,1)S(1)} fusion(bf16[1024,640]{1,0:T(8,128)(2,1)} %get-tuple-element.668, f32[192,640]{1,0:T(8,128)S(1)} %get-tuple-element.616, bf16[1,2,192,640]{3,2,1,0:T(8,128)(2,1)S(1)} %copy-done.4, s32[]{:T(128)S(6)} %min.13), kind=kOutput, calls=%fused_computation.62.clone.1 | convolution fusion | flops 253206528 | bytes 2441220 | tf_op jit(solution)/shard_map/while/body/eval_jaxpr/dot_general | solution.py:39
  92.0 0.9 reshape.170
  93.0 4.2 %all-to-all-done.2 = bf16[32,1,6]{2,1,0:T(2,128)(2,1)S(1)} async-done(((bf16[32,1,6]{2,1,0:T(2,128)(2,1)}), bf16[32,1,6]{2,1,0:T(2,128)(2,1)S(1)}, u32[]{:S(2)}, u32[]{:S(2)}) %all-to-all-start.2) | async-done | bytes 416 | tf_op jit(solution)/shard_map/while/body/eval_jaxpr/all_to_all | solution.py:57
  97.2 2.6 %all-to-all-start.1 = ((bf16[32,6,1024]{2,1,0:T(8,128)(2,1)}), bf16[32,6,1024]{2,1,0:T(8,128)(2,1)S(1)}, u32[]{:S(2)}, u32[]{:S(2)}) async-start(bf16[32,6,1024]{2,1,0:T(8,128)(2,1)} %reshape.170), calls=%async_computation.1 | async-start | bytes 1048576 | tf_op jit(solution)/shard_map/while/body/eval_jaxpr/all_to_all | solution.py:54
  100.5 14.9 %all-to-all-done.1 = bf16[32,6,1024]{2,1,0:T(8,128)(2,1)S(1)} async-done(((bf16[32,6,1024]{2,1,0:T(8,128)(2,1)}), bf16[32,6,1024]{2,1,0:T(8,128)(2,1)S(1)}, u32[]{:S(2)}, u32[]{:S(2)}) %all-to-all-start.1) | async-done | bytes 393248 | tf_op jit(solution)/shard_map/while/body/eval_jaxpr/all_to_all | solution.py:54
  116.9 2.4 %fusion.206 = bf16[2,128,1024]{2,1,0:T(8,128)(2,1)S(1)} fusion(bf16[2,128,1024]{2,1,0:T(8,128)(2,1)S(1)} %get-tuple-element.641, s32[]{:T(128)S(6)} %min.13, pred[]{:T(512)S(6)} %ge.12, f32[128,1024]{1,0:T(8,128)S(1)} %multiply_multiply_fusion.5, f32[1024]{0:T(1024)S(1)} %bitcast.188, f32[1024]{0:T(1024)S(1)} %bitcast.226, f32[1024]{0:T(1024)S(1)} %bitcast.250, ...), kind=kLoop, calls=%fused_computation.223.clone.1 | loop fusion | flops 9568256 | bytes 2492421 | tf_op jit(solution)/shard_map/while/body/eval_jaxpr/jit(_where)/select_n | solution.py:172
  119.3 0.8 copy-done.3
  (58 shorter events, 8.7 us)
Async XLA Ops:
  2.3 9.6 %copy-start.5 = (s32[2,1]{0,1:T(1,128)S(1)}, s32[2,1]{0,1:T(1,128)}, u32[]{:S(2)}) copy-start(s32[2,1]{0,1:T(1,128)} %get-tuple-element.660) | copy-start | bytes 28 | tf_op jit(solution)/shard_map/while
  2.3 10.8 %copy-start.1 = (bf16[1,2,128,1024]{3,2,1,0:T(8,128)(2,1)S(1)}, bf16[1,2,128,1024]{3,2,1,0:T(8,128)(2,1)}, u32[]{:S(2)}) copy-start(bf16[1,2,128,1024]{3,2,1,0:T(8,128)(2,1)} %get-tuple-element.659) | copy-start | bytes 1572868 | tf_op jit(solution)/shard_map/while
  4.5 22.9 %all-to-all-start = ((bf16[32,6,1024]{2,1,0:T(8,128)(2,1)}), bf16[32,6,1024]{2,1,0:T(8,128)(2,1)S(1)}, u32[]{:S(2)}, u32[]{:S(2)}) async-start(bf16[32,6,1024]{2,1,0:T(8,128)(2,1)} %reshape.168), calls=%async_computation | async-start | bytes 1048576 | tf_op jit(solution)/shard_map/while/body/eval_jaxpr/all_to_all | solution.py:45
  13.2 14.3 %copy-start.4 = (bf16[1,2,192,640]{3,2,1,0:T(8,128)(2,1)S(1)}, bf16[1,2,192,640]{3,2,1,0:T(8,128)(2,1)}, u32[]{:S(2)}) copy-start(bf16[1,2,192,640]{3,2,1,0:T(8,128)(2,1)} %get-tuple-element.667) | copy-start | bytes 1474564 | tf_op jit(solution)/shard_map/while
  30.3 10.2 %all-to-all-start.2 = ((bf16[32,1,6]{2,1,0:T(2,128)(2,1)}), bf16[32,1,6]{2,1,0:T(2,128)(2,1)S(1)}, u32[]{:S(2)}, u32[]{:S(2)}) async-start(bf16[32,1,6]{2,1,0:T(2,128)(2,1)} %convert_element_type.234), calls=%async_computation.2 | async-start | bytes 32768 | tf_op jit(solution)/shard_map/while/body/eval_jaxpr/all_to_all | solution.py:57
  35.3 7.8 %copy-start.2 = (bf16[32,1024]{1,0:T(8,128)(2,1)S(1)}, bf16[32,1024]{1,0:T(8,128)(2,1)}, u32[]{:S(2)}) copy-start(bf16[32,1024]{1,0:T(8,128)(2,1)} %get-tuple-element.663) | copy-start | bytes 196612 | tf_op jit(solution)/shard_map/while
  40.5 18.2 %all-to-all-start.1 = ((bf16[32,6,1024]{2,1,0:T(8,128)(2,1)}), bf16[32,6,1024]{2,1,0:T(8,128)(2,1)S(1)}, u32[]{:S(2)}, u32[]{:S(2)}) async-start(bf16[32,6,1024]{2,1,0:T(8,128)(2,1)} %reshape.170), calls=%async_computation.1 | async-start | bytes 1048576 | tf_op jit(solution)/shard_map/while/body/eval_jaxpr/all_to_all | solution.py:54
  58.8 1.0 copy-start
  63.3 5.3 %copy-start.5 = (s32[2,1]{0,1:T(1,128)S(1)}, s32[2,1]{0,1:T(1,128)}, u32[]{:S(2)}) copy-start(s32[2,1]{0,1:T(1,128)} %get-tuple-element.660) | copy-start | bytes 28 | tf_op jit(solution)/shard_map/while
  63.3 6.5 %copy-start.1 = (bf16[1,2,128,1024]{3,2,1,0:T(8,128)(2,1)S(1)}, bf16[1,2,128,1024]{3,2,1,0:T(8,128)(2,1)}, u32[]{:S(2)}) copy-start(bf16[1,2,128,1024]{3,2,1,0:T(8,128)(2,1)} %get-tuple-element.659) | copy-start | bytes 1572868 | tf_op jit(solution)/shard_map/while
  65.5 18.5 %all-to-all-start = ((bf16[32,6,1024]{2,1,0:T(8,128)(2,1)}), bf16[32,6,1024]{2,1,0:T(8,128)(2,1)S(1)}, u32[]{:S(2)}, u32[]{:S(2)}) async-start(bf16[32,6,1024]{2,1,0:T(8,128)(2,1)} %reshape.168), calls=%async_computation | async-start | bytes 1048576 | tf_op jit(solution)/shard_map/while/body/eval_jaxpr/all_to_all | solution.py:45
  69.9 14.3 %copy-start.4 = (bf16[1,2,192,640]{3,2,1,0:T(8,128)(2,1)S(1)}, bf16[1,2,192,640]{3,2,1,0:T(8,128)(2,1)}, u32[]{:S(2)}) copy-start(bf16[1,2,192,640]{3,2,1,0:T(8,128)(2,1)} %get-tuple-element.667) | copy-start | bytes 1474564 | tf_op jit(solution)/shard_map/while
  87.0 10.2 %all-to-all-start.2 = ((bf16[32,1,6]{2,1,0:T(2,128)(2,1)}), bf16[32,1,6]{2,1,0:T(2,128)(2,1)S(1)}, u32[]{:S(2)}, u32[]{:S(2)}) async-start(bf16[32,1,6]{2,1,0:T(2,128)(2,1)} %convert_element_type.234), calls=%async_computation.2 | async-start | bytes 32768 | tf_op jit(solution)/shard_map/while/body/eval_jaxpr/all_to_all | solution.py:57
  92.0 7.8 %copy-start.2 = (bf16[32,1024]{1,0:T(8,128)(2,1)S(1)}, bf16[32,1024]{1,0:T(8,128)(2,1)}, u32[]{:S(2)}) copy-start(bf16[32,1024]{1,0:T(8,128)(2,1)} %get-tuple-element.663) | copy-start | bytes 196612 | tf_op jit(solution)/shard_map/while
  97.2 18.2 %all-to-all-start.1 = ((bf16[32,6,1024]{2,1,0:T(8,128)(2,1)}), bf16[32,6,1024]{2,1,0:T(8,128)(2,1)S(1)}, u32[]{:S(2)}, u32[]{:S(2)}) async-start(bf16[32,6,1024]{2,1,0:T(8,128)(2,1)} %reshape.170), calls=%async_computation.1 | async-start | bytes 1048576 | tf_op jit(solution)/shard_map/while/body/eval_jaxpr/all_to_all | solution.py:54
  115.5 1.0 copy-start
  119.3 0.8 copy-start.3
where the time goes:
time: 121 us; the launch traced here: 120 us
  waiting for transfers between devices  58.5 us (48%)
  starting transfers between devices  21.6 us (18%)
  other arithmetic  17.9 us (15%)
  matrix products  12.7 us (10%)
  local copies, waits for them, and re-layouts  8.88 us (7%)
    all_to_all x2, waiting for transfers between devices, expert_whole(): lax.all_to_all(slot_grad.reshape(recv_shape), 'expert', split_axis=0, con...  29.8 us
    all_to_all x2, waiting for transfers between devices, expert_whole(): lax.all_to_all(bucket, 'expert', split_axis=0, concat_axis=0, tiled=True)  20.3 us
    all_to_all x2, starting transfers between devices, expert_whole(): lax.all_to_all(bucket, 'expert', split_axis=0, concat_axis=0, tiled=True)  10.3 us
    all_to_all x2, waiting for transfers between devices, expert_whole(): lax.all_to_all(gate_grad.reshape(recv_shape[0], recv_shape[1]).astype(jnp...  8.48 us
    reduce_sum x2, other arithmetic, block_grad(): jnp.mean(residual * residual, axis=1, keepdims=True) + 1e-06  7.99 us
    dot_general x4, matrix products, contract_last(): lax.dot_general(left, right, (((1,), (1,)), ((), ())), preferred_element_...  7.97 us
    all_to_all x2, starting transfers between devices, expert_whole(): lax.all_to_all(gate_grad.reshape(recv_shape[0], recv_shape[1]).astype(jnp...  6.15 us
    all_to_all x2, starting transfers between devices, expert_whole(): lax.all_to_all(slot_grad.reshape(recv_shape), 'expert', split_axis=0, con...  5.21 us
  transfers between devices with their start and end apart: 6, of which 6 were waited for; matrix products, arithmetic and copies ran while one was open for 15% of the time, Pallas kernels for 0%

commit v1 on v0

v1 whole, which is shorter than its diff:
```python
import functools
import math

import jax
import jax.numpy as jnp
from jax import lax
from jax.experimental import pallas as pl
from jax.experimental.pallas import tpu as pltpu
from jax.sharding import PartitionSpec as P

LANES = 128
SUB = 8
MESH = pl.DeviceIdType.MESH


def contract_last(left, right):
    return lax.dot_general(
        left, right, (((1,), (1,)), ((), ())), preferred_element_type=jnp.float32
    )


def to_column(row):
    size = row.shape[1]
    same = lax.broadcasted_iota(jnp.int32, (size, size), 0) == lax.broadcasted_iota(
        jnp.int32, (size, size), 1
    )
    wide = jnp.broadcast_to(row.astype(jnp.float32), (size, size))
    return jnp.sum(jnp.where(same, wide, 0.0), axis=1, keepdims=True).astype(jnp.int32)


def kernel(
    axis,
    n,
    slot_cap,
    length_ref,
    routed_ref,
    slot_ref,
    conv_ref,
    gain_ref,
    cent_ref,
    feat_hbm,
    grad_hbm,
    preact_hbm,
    w_in_hbm,
    w_out_hbm,
    out_hbm,
    feat_ref,
    grad_ref,
    preact_ref,
    w_in_ref,
    w_out_ref,
    out_ref,
    taps_ref,
    gain_f,
    send_ref,
    recv_ref,
    back_ref,
    home_ref,
    gate_send,
    gate_recv,
    turn_ref,
    rows_ref,
    pad_ref,
    resid_ref,
    slope_ref,
    cent_rows,
    gelu_ref,
    gelu_slope_ref,
    slot_back,
    load_sem,
    out_sem,
    send_sem,
    recv_sem,
    back_sem,
    home_sem,
    gate_send_sem,
    gate_recv_sem,
):
    micro, frames, width = feat_ref.shape
    chunks = width // LANES
    slots = n * slot_cap
    tap_count = conv_ref.shape[0]
    low = tap_count // 2
    experts = n
    gate_span = LANES // micro
    me = lax.axis_index(axis)

    barrier = pltpu.get_barrier_semaphore()

    def greet(step, carry):
        pl.semaphore_signal(
            barrier, inc=1, device_id={axis: lax.rem(me + step, n)}, device_id_type=MESH
        )
        return carry

    def load(src, dst, at):
        return pltpu.make_async_copy(src, dst, load_sem.at[at])

    grad_loads = [load(grad_hbm.at[m], grad_ref.at[m], m) for m in range(micro)]
    feat_loads = [load(feat_hbm.at[m], feat_ref.at[m], micro + m) for m in range(micro)]
    pre_load = load(preact_hbm, preact_ref, 2 * micro)
    out_load = load(w_out_hbm, w_out_ref, 2 * micro + 1)
    in_load = load(w_in_hbm, w_in_ref, 2 * micro + 2)
    for copy in (*grad_loads, *feat_loads, pre_load, out_load, in_load):
        copy.start()
    lax.fori_loop(1, n, greet, 0)

    def cols(c):
        return pl.ds(c * LANES, LANES)

    def to_blocks(rows, dst):
        for c in range(chunks):
            turn_ref[pl.ds(c, slots, stride=chunks), :] = rows[:, c * LANES : (c + 1) * LANES]
        dst[...] = turn_ref[...].astype(jnp.bfloat16).reshape(dst.shape)

    def from_blocks(src):
        turn_ref[...] = src[...].reshape(turn_ref.shape).astype(jnp.float32)
        for c in range(chunks):
            rows_ref[:, cols(c)] = turn_ref[pl.ds(c, slots, stride=chunks), :].astype(jnp.bfloat16)

    def exchange(src, dst, sent, got):
        def post(step, carry):
            peer = lax.rem(me + step, n)
            pltpu.make_async_remote_copy(
                src_ref=src.at[peer],
                dst_ref=dst.at[me],
                send_sem=sent,
                recv_sem=got,
                device_id={axis: peer},
                device_id_type=MESH,
            ).start()
            return carry

        lax.fori_loop(1, n, post, 0)
        pltpu.make_async_copy(src.at[me], dst.at[me], got).start()

    def arrived(dst, got):
        pltpu.make_async_copy(dst, dst, got).wait()

    def departed(src, sent):
        part = src.at[pl.ds(0, n - 1)]
        pltpu.make_async_copy(part, part, sent).wait()

    for m in range(micro):
        grad_loads[m].wait()
        target = routed_ref[m : m + 1, :] * slot_cap + slot_ref[m : m + 1, :]
        onehot = (lax.broadcasted_iota(jnp.int32, (slots, frames), 0) == target).astype(
            jnp.float32
        ).astype(jnp.bfloat16)
        bucket = jnp.dot(onehot, grad_ref[m], preferred_element_type=jnp.float32)
        to_blocks(bucket, send_ref.at[m])
        if m == 0:
            pl.semaphore_wait(barrier, n - 1)
        exchange(send_ref.at[m], recv_ref.at[m], send_sem.at[m], recv_sem.at[m])

    for c in range(chunks):
        taps_ref[c] = conv_ref[:, cols(c)].astype(jnp.float32)
        gain_f[c] = gain_ref[:, cols(c)].astype(jnp.float32)
        pad_ref[c, 0:low, :] = jnp.zeros((low, LANES), jnp.float32)
        pad_ref[c, low + frames :, :] = jnp.zeros((tap_count - low, LANES), jnp.float32)

    frame_at = lax.broadcasted_iota(jnp.int32, (frames, 1), 0)

    masks, inv_all, gate_all, exp_all, slot_all, slot_hot = [], [], [], [], [], []
    for m in range(micro):
        feat_loads[m].wait()
        mask = (frame_at < length_ref[m, 0]).astype(jnp.float32)
        routed = to_column(routed_ref[m : m + 1, :])
        slot_pos = to_column(slot_ref[m : m + 1, :])
        exp_hot = (
            lax.broadcasted_iota(jnp.int32, (frames, experts), 1) == routed
        ).astype(jnp.float32)
        cent_rows[m] = jnp.dot(
            exp_hot.astype(jnp.bfloat16), cent_ref[...], preferred_element_type=jnp.float32
        ).astype(jnp.bfloat16)

        def ahead(c, square):
            lanes = pl.ds(pl.multiple_of(c * LANES, LANES), LANES)
            feats = feat_ref[m, :, lanes].astype(jnp.float32)
            pad_ref[c, low : low + frames, :] = feats * mask
            acc = jnp.zeros((frames, LANES), jnp.float32)
            for k in range(tap_count):
                acc = acc + taps_ref[c, k : k + 1, :] * pad_ref[c, k : k + frames, :]
            sig = jax.nn.sigmoid(acc)
            resid = feats + mask * acc * sig
            resid_ref[m, c] = resid
            slope_ref[m, c] = mask * sig * (1.0 + acc * (1.0 - sig))
            return square + resid * resid

        square = lax.fori_loop(0, chunks, ahead, jnp.zeros((frames, LANES), jnp.float32))
        inv_rms = lax.rsqrt(jnp.sum(square, axis=1, keepdims=True) * (1.0 / width) + 1e-06)

        def scoring(c, total):
            lanes = pl.ds(pl.multiple_of(c * LANES, LANES), LANES)
            normed = (resid_ref[m, c] * inv_rms * gain_f[c]).astype(jnp.bfloat16)
            return total + normed.astype(jnp.float32) * cent_rows[m, :, lanes].astype(jnp.float32)

        score = lax.fori_loop(0, chunks, scoring, jnp.zeros((frames, LANES), jnp.float32))
        gate_all.append(jax.nn.sigmoid(jnp.sum(score, axis=1, keepdims=True)))
        masks.append(mask)
        inv_all.append(inv_rms)
        exp_all.append(exp_hot)
        slot_all.append(slot_pos)
        slot_hot.append(
            (
                lax.broadcasted_iota(jnp.int32, (frames, slots), 1)
                == routed * slot_cap + slot_pos
            ).astype(jnp.float32).astype(jnp.bfloat16)
        )

        if m == 0:
            pre_load.wait()
        act = preact_ref[m].astype(jnp.float32)
        cdf = 0.5 * (1.0 + lax.erf(act * (1.0 / math.sqrt(2.0))))
        gelu_ref[m] = act * cdf
        gelu_slope_ref[m] = cdf + act * jnp.exp(-0.5 * act * act) * (
            1.0 / math.sqrt(2.0 * math.pi)
        )

    out_load.wait()
    in_load.wait()
    gate_rows = jnp.zeros((n, LANES), jnp.float32)
    slot_id = lax.broadcasted_iota(jnp.int32, (slots, LANES), 0)
    lane_id = lax.broadcasted_iota(jnp.int32, (slots, LANES), 1)
    group_first = lax.broadcasted_iota(jnp.int32, (n, slots), 0) * slot_cap
    group_slot = lax.broadcasted_iota(jnp.int32, (n, slots), 1)
    grouped = jnp.logical_and(
        group_slot >= group_first, group_slot < group_first + slot_cap
    ).astype(jnp.float32)
    for m in range(micro):
        arrived(recv_ref.at[m], recv_sem.at[m])
        from_blocks(recv_ref.at[m])
        hidden = contract_last(rows_ref[...], w_out_ref[...])
        gate = jnp.sum(hidden * gelu_ref[m], axis=1, keepdims=True)
        pre_grad = (hidden * gelu_slope_ref[m]).astype(jnp.bfloat16)
        to_blocks(contract_last(pre_grad, w_in_ref[...]), back_ref.at[m])
        exchange(back_ref.at[m], home_ref.at[m], back_sem.at[m], home_sem.at[m])
        spread = jnp.where(lax.rem(slot_id, slot_cap) + m * gate_span == lane_id, gate, 0.0)
        gate_rows = gate_rows + jnp.dot(
            grouped, spread, preferred_element_type=jnp.float32, precision=lax.Precision.HIGHEST
        )
    gate_send[...] = gate_rows.reshape(gate_send.shape)
    exchange(gate_send, gate_recv, gate_send_sem, gate_recv_sem)
    arrived(gate_recv, gate_recv_sem)
    gate_home = gate_recv[...].reshape(n, LANES)

    frame_lane = lax.broadcasted_iota(jnp.int32, (frames, LANES), 1)
    for m in range(micro):
        mask, inv_rms, gate_val = masks[m], inv_all[m], gate_all[m]
        picked = jnp.dot(
            exp_all[m],
            gate_home,
            preferred_element_type=jnp.float32,
            precision=lax.Precision.HIGHEST,
        )
        gate_grad = jnp.sum(
            jnp.where(frame_lane == slot_all[m] + m * gate_span, picked, 0.0),
            axis=1,
            keepdims=True,
        )
        cent_scale = gate_val * (1.0 - gate_val) * gate_grad
        arrived(home_ref.at[m], home_sem.at[m])
        from_blocks(home_ref.at[m])
        slot_back[...] = jnp.dot(slot_hot[m], rows_ref[...], preferred_element_type=jnp.float32)

        def scaling(c, total):
            lanes = pl.ds(pl.multiple_of(c * LANES, LANES), LANES)
            grad = gate_val * slot_back[:, lanes] + cent_scale * cent_rows[m, :, lanes].astype(
                jnp.float32
            )
            scaled = grad * gain_f[c]
            slot_back[:, lanes] = scaled
            return total + resid_ref[m, c] * scaled

        total = lax.fori_loop(0, chunks, scaling, jnp.zeros((frames, LANES), jnp.float32))
        mean = jnp.sum(total, axis=1, keepdims=True) * (1.0 / width)
        back_scale = inv_rms * inv_rms * inv_rms * mean

        def finish(c, carry):
            lanes = pl.ds(pl.multiple_of(c * LANES, LANES), LANES)
            resid_grad = (
                grad_ref[m, :, lanes].astype(jnp.float32)
                + inv_rms * slot_back[:, lanes]
                - resid_ref[m, c] * back_scale
            )
            pad_ref[c, low : low + frames, :] = slope_ref[m, c] * resid_grad
            acc = jnp.zeros((frames, LANES), jnp.float32)
            for k in range(tap_count):
                first = 2 * low - k
                acc = acc + taps_ref[c, k : k + 1, :] * pad_ref[c, first : first + frames, :]
            out_ref[m, :, lanes] = (resid_grad + mask * acc).astype(jnp.bfloat16)
            return carry

        lax.fori_loop(0, chunks, finish, 0)
        pltpu.make_async_copy(out_ref.at[m], out_hbm.at[m], out_sem.at[m]).start()

    for m in range(micro):
        departed(send_ref.at[m], send_sem.at[m])
        departed(back_ref.at[m], back_sem.at[m])
    departed(gate_send, gate_send_sem)
    for m in range(micro):
        pltpu.make_async_copy(out_ref.at[m], out_hbm.at[m], out_sem.at[m]).wait()


def block_grads(
    grads, feats, lengths, routed, slot_pos, preact, conv_k, gain, cent, weight_in, weight_out
):
    micro, frames, width = feats.shape
    n = lax.axis_size("expert")
    hidden = weight_in.shape[1]
    cap = preact.shape[1] // n
    whole_rows = 16 * LANES // math.gcd(16 * LANES, width)
    slot_cap = -(-cap // whole_rows) * whole_rows
    if slot_cap != cap:
        preact = jnp.pad(
            preact.reshape(micro, n, cap, hidden), ((0, 0), (0, 0), (0, slot_cap - cap), (0, 0))
        ).reshape(micro, n * slot_cap, hidden)
    slots = n * slot_cap
    chunks = width // LANES
    taps = conv_k.shape[0]
    block = (n, slot_cap * chunks, LANES)
    bf16, f32 = jnp.bfloat16, jnp.float32
    vmem = pl.BlockSpec(memory_space=pltpu.VMEM)
    smem = pl.BlockSpec(memory_space=pltpu.SMEM)
    anywhere = pl.BlockSpec(memory_space=pl.ANY)
    dma = pltpu.SemaphoreType.DMA
    flops = micro * (4 * slots * width * hidden + 4 * frames * width * (taps + slots))
    return pl.pallas_call(
        functools.partial(kernel, "expert", n, slot_cap),
        out_shape=jax.ShapeDtypeStruct((micro, frames, width), bf16),
        in_specs=[smem] + [vmem] * 5 + [anywhere] * 5,
        out_specs=anywhere,
        scratch_shapes=[
            pltpu.VMEM((micro, frames, width), bf16),
            pltpu.VMEM((micro, frames, width), bf16),
            pltpu.VMEM((micro, slots, hidden), bf16),
            pltpu.VMEM((width, hidden), bf16),
            pltpu.VMEM((hidden, width), bf16),
            pltpu.VMEM((micro, frames, width), bf16),
            pltpu.VMEM((chunks, taps, LANES), f32),
            pltpu.VMEM((chunks, 1, LANES), f32),
            pltpu.VMEM((micro, *block), bf16),
            pltpu.VMEM((micro, *block), bf16),
            pltpu.VMEM((micro, *block), bf16),
            pltpu.VMEM((micro, *block), bf16),
            pltpu.VMEM((n, 1, LANES), f32),
            pltpu.VMEM((n, 1, LANES), f32),
            pltpu.VMEM((slots * chunks, LANES), f32),
            pltpu.VMEM((slots, width), bf16),
            pltpu.VMEM((chunks, frames + taps, LANES), f32),
            pltpu.VMEM((micro, chunks, frames, LANES), f32),
            pltpu.VMEM((micro, chunks, frames, LANES), f32),
            pltpu.VMEM((micro, frames, width), bf16),
            pltpu.VMEM((micro, slots, hidden), f32),
            pltpu.VMEM((micro, slots, hidden), f32),
            pltpu.VMEM((frames, width), f32),
            dma((2 * micro + 3,)),
            dma((micro,)),
            dma((micro,)),
            dma((micro,)),
            dma((micro,)),
            dma((micro,)),
            dma,
            dma,
        ],
        compiler_params=pltpu.CompilerParams(
            collective_id=0, has_side_effects=True, vmem_limit_bytes=40 * 1024 * 1024
        ),
        cost_estimate=pl.CostEstimate(
            flops=flops, bytes_accessed=8 * 1024 * 1024, transcendentals=0
        ),
    )(lengths, routed, slot_pos, conv_k, gain, cent, feats, grads, preact, weight_in, weight_out)


def on_device(
    feat_saved,
    out_grad,
    lengths,
    expert_ids,
    slot_ids,
    expert_preact,
    conv_weight,
    norm_gain,
    centroids,
    w_in,
    w_out,
):
    section_count = lax.axis_size("section")
    micro_count = out_grad.shape[0]
    feats, routed, slots, preact = feat_saved[0], expert_ids[0], slot_ids[0], expert_preact[0]
    fixed = (conv_weight[0], norm_gain, centroids[0], w_in[0, 0], w_out[0, 0])
    if section_count == 1:
        return block_grads(out_grad, feats, lengths, routed, slots, preact, *fixed)[None]

    section_idx = lax.axis_index("section")
    route = [(i + 1, i) for i in range(section_count - 1)]

    def one_tick(tick_idx, carry):
        incoming, grads = carry
        micro_pos = tick_idx - (section_count - 1 - section_idx)
        is_valid = jnp.logical_and(micro_pos >= 0, micro_pos < micro_count)
        micro_sel = jnp.clip(micro_pos, 0, micro_count - 1)

        def pick(array):
            return lax.dynamic_slice_in_dim(array, micro_sel, 1, 0)

        grad_in = jnp.where(section_idx == section_count - 1, pick(out_grad), incoming)
        new_grad = block_grads(
            grad_in, pick(feats), pick(lengths), pick(routed), pick(slots), pick(preact), *fixed
        )
        updated = lax.dynamic_update_slice_in_dim(grads, new_grad, micro_sel, 0)
        grads = jnp.where(is_valid, updated, grads)
        return (lax.ppermute(new_grad, "section", route), grads)

    start = (jnp.zeros((1, *out_grad.shape[1:]), jnp.bfloat16), jnp.zeros_like(out_grad))
    _, grads = lax.fori_loop(0, section_count + micro_count - 1, one_tick, start)
    return grads[None]


def solution(mesh):
    in_specs = (
        P("section", None, "expert", None),
        P(None, "expert", None),
        P(None, "expert"),
        P("section", None, "expert"),
        P("section", None, "expert"),
        P("section", None, "expert", None),
        P("section", None, None),
        P("section", None),
        P("section", None, None),
        P("section", "expert", None, None),
        P("section", "expert", None, None),
    )
    out_specs = P("section", None, "expert", None)
    return jax.shard_map(
        on_device, mesh=mesh, in_specs=in_specs, out_specs=out_specs, check_vma=False
    )
```

time: 121 us -> 60.8 us (0.50)
  waiting for transfers between devices: 58.5 us -> 0 us
  Pallas kernels: 0 us -> 49.3 us
  starting transfers between devices: 21.6 us -> 0 us
  other arithmetic: 17.9 us -> 0 us
  matrix products: 12.7 us -> 0 us
  local copies, waits for them, and re-layouts: 8.88 us -> 11 us
    all_to_all x6 -> x0, waiting for transfers between devices: 58.5 us -> none  [the longest x2 29.8 us: expert_whole(): lax.all_to_all(slot_grad.reshape(recv_shape), 'expert', split_axis=0, con...]
    pallas_call x0 -> x1, Pallas kernels: none -> 49.3 us  [block_grads(): pl.pallas_call(functools.partial(kernel, 'expert', n, slot_cap), out_shap...]
    all_to_all x6 -> x0, starting transfers between devices: 21.6 us -> none  [the longest x2 10.3 us: expert_whole(): lax.all_to_all(bucket, 'expert', split_axis=0, concat_axis=0, tiled=True)]
    dot_general x14 -> x0, matrix products: 12.7 us -> none  [the longest x4 7.97 us: contract_last(): lax.dot_general(left, right, (((1,), (1,)), ((), ())), preferred_element_...]
    unnamed x2 -> x22, local copies, waits for them, and re-layouts: 0.79 us -> 11 us
    reduce_sum x2 -> x0, other arithmetic: 7.99 us -> none  [block_grad(): jnp.mean(residual * residual, axis=1, keepdims=True) + 1e-06]
    select_n x2 -> x0, other arithmetic: 4.81 us -> none  [one_tick(): grads = jnp.where(is_valid, updated, grads)]
    reshape x10 -> x0, local copies, waits for them, and re-layouts: 4.46 us -> none  [the longest x2 1.85 us: expert_whole(): slot_grad.reshape(recv_shape)]
  transfers between devices with their start and end apart: 6 -> 0, of which waited for: 6 -> 0; matrix products, arithmetic and copies ran while one was open for 15% -> 0% of each run, Pallas kernels for 0% -> 0%
where the time goes in v1:
time: 60.8 us; the launch traced here: 60.3 us
  Pallas kernels  49.3 us (81%)
  local copies, waits for them, and re-layouts  11 us (18%)
    pallas_call x1, Pallas kernels, block_grads(): pl.pallas_call(functools.partial(kernel, 'expert', n, slot_cap), out_shap...  49.3 us
    unnamed x22, local copies, waits for them, and re-layouts  11 us

profile of v1, /device:TPU:0, one launch (start us, length us, event | category | flops | bytes accessed | tf_op | source)
XLA Modules:
  0.0 60.3 jit_solution(7073899929176116941)
XLA Ops:
  0.0 0.7 %copy.12.length_ref = s32[2,1]{1,0:T(2,128)S(1)} copy(s32[2,1]{0,1:T(1,128)} %param.13) | data formatting | bytes 16 | tf_op args[2]
  0.7 0.0 copy-start
  0.7 1.3 %copy-done = bf16[1,1,1024,640]{3,2,1,0:T(8,128)(2,1)S(1)} copy-done((bf16[1,1,1024,640]{3,2,1,0:T(8,128)(2,1)S(1)}, bf16[1,1,1024,640]{3,2,1,0:T(8,128)(2,1)}, u32[]{:S(2)}) %copy-start) | copy-done | bytes 1310744
  2.1 0.0 copy-start.1
  2.1 1.3 %copy-done.1 = bf16[1,1,640,1024]{3,2,1,0:T(8,128)(2,1)S(1)} copy-done((bf16[1,1,640,1024]{3,2,1,0:T(8,128)(2,1)S(1)}, bf16[1,1,640,1024]{3,2,1,0:T(8,128)(2,1)}, u32[]{:S(2)}) %copy-start.1) | copy-done | bytes 1310744
  3.4 0.0 copy-start.2
  3.4 1.0 %copy-done.2 = bf16[1,2,128,1024]{3,2,1,0:T(8,128)(2,1)S(1)} copy-done((bf16[1,2,128,1024]{3,2,1,0:T(8,128)(2,1)S(1)}, bf16[1,2,128,1024]{3,2,1,0:T(8,128)(2,1)}, u32[]{:S(2)}) %copy-start.2) | copy-done | bytes 524312
  4.4 0.0 copy-start.3
  4.4 1.0 %copy-done.3 = bf16[2,128,1024]{2,1,0:T(8,128)(2,1)S(1)} copy-done((bf16[2,128,1024]{2,1,0:T(8,128)(2,1)S(1)}, bf16[2,128,1024]{2,1,0:T(8,128)(2,1)}, u32[]{:S(2)}) %copy-start.3) | copy-done | bytes 524312
  5.5 0.0 copy-start.4
  5.5 1.0 %copy-done.4 = bf16[1,2,192,640]{3,2,1,0:T(8,128)(2,1)S(1)} copy-done((bf16[1,2,192,640]{3,2,1,0:T(8,128)(2,1)S(1)}, bf16[1,2,192,640]{3,2,1,0:T(8,128)(2,1)}, u32[]{:S(2)}) %copy-start.4) | copy-done | bytes 491544
  6.5 0.0 copy-start.5
  6.5 0.8 %copy-done.5 = bf16[1,32,1024]{2,1,0:T(8,128)(2,1)S(1)} copy-done((bf16[1,32,1024]{2,1,0:T(8,128)(2,1)S(1)}, bf16[1,32,1024]{2,1,0:T(8,128)(2,1)}, u32[]{:S(2)}) %copy-start.5) | copy-done | bytes 65560
  7.3 0.0 copy-start.6
  7.3 0.8 %copy-done.6 = bf16[1,32,1024]{2,1,0:T(8,128)(2,1)S(1)} copy-done((bf16[1,32,1024]{2,1,0:T(8,128)(2,1)S(1)}, bf16[1,32,1024]{2,1,0:T(8,128)(2,1)}, u32[]{:S(2)}) %copy-start.6) | copy-done | bytes 65560
  8.2 0.0 copy-start.7
  8.2 0.7 %copy-done.7 = bf16[1,1024]{1,0:T(2,128)(2,1)S(1)} copy-done((bf16[1,1024]{1,0:T(2,128)(2,1)S(1)}, bf16[1,1024]{1,0:T(2,128)(2,1)}, u32[]{:S(2)}) %copy-start.7) | copy-done | bytes 2072
  8.9 0.0 copy-start.8
  8.9 0.7 %copy-done.8 = s32[1,2,128]{2,1,0:T(2,128)S(1)} copy-done((s32[1,2,128]{2,1,0:T(2,128)S(1)}, s32[1,2,128]{2,1,0:T(2,128)}, u32[]{:S(2)}) %copy-start.8) | copy-done | bytes 1048
  9.5 0.0 copy-start.9
  9.5 0.7 %copy-done.9 = s32[1,2,128]{2,1,0:T(2,128)S(1)} copy-done((s32[1,2,128]{2,1,0:T(2,128)S(1)}, s32[1,2,128]{2,1,0:T(2,128)}, u32[]{:S(2)}) %copy-start.9) | copy-done | bytes 1048
  10.2 49.3 %shard_map.109 = bf16[2,128,1024]{2,1,0:T(8,128)(2,1)S(1)} custom-call(s32[2,1]{1,0:T(2,128)S(1)} %copy.12.length_ref, s32[2,128]{1,0:T(2,128)S(1)} %bitcast.16, s32[2,128]{1,0:T(2,128)S(1)} %bitcast.17, bf16[32,1024]{1,0:T(8,128)(2,1)S(1)} %bitcast.14, bf16[1,1024]{1,0:T(2,128)(2,1)S(1)} %copy-done.7, bf16[32,1024]{1,0:T(8,128)(2,1)S(1)} %bitcast.15, ...), custom_call_target="tpu_custom_call" | custom-call | flops 1241513984 | bytes 8388608 | tf_op jit(solution)/shard_map/pallas_call | solution.py:328
  59.5 0.8 %copy.14 = bf16[1,2,128,1024]{3,2,1,0:T(8,128)(2,1)} copy(bf16[1,2,128,1024]{3,2,1,0:T(8,128)(2,1)S(1)} %bitcast.9) | data formatting | bytes 1048576
Async XLA Ops:
  0.7 1.3 %copy-start = (bf16[1,1,1024,640]{3,2,1,0:T(8,128)(2,1)S(1)}, bf16[1,1,1024,640]{3,2,1,0:T(8,128)(2,1)}, u32[]{:S(2)}) copy-start(bf16[1,1,1024,640]{3,2,1,0:T(8,128)(2,1)} %param.20) | copy-start | bytes 3932164
  2.1 1.3 %copy-start.1 = (bf16[1,1,640,1024]{3,2,1,0:T(8,128)(2,1)S(1)}, bf16[1,1,640,1024]{3,2,1,0:T(8,128)(2,1)}, u32[]{:S(2)}) copy-start(bf16[1,1,640,1024]{3,2,1,0:T(8,128)(2,1)} %param.21) | copy-start | bytes 3932164
  3.4 1.0 %copy-start.2 = (bf16[1,2,128,1024]{3,2,1,0:T(8,128)(2,1)S(1)}, bf16[1,2,128,1024]{3,2,1,0:T(8,128)(2,1)}, u32[]{:S(2)}) copy-start(bf16[1,2,128,1024]{3,2,1,0:T(8,128)(2,1)} %param.11) | copy-start | bytes 1572868
  4.4 1.0 %copy-start.3 = (bf16[2,128,1024]{2,1,0:T(8,128)(2,1)S(1)}, bf16[2,128,1024]{2,1,0:T(8,128)(2,1)}, u32[]{:S(2)}) copy-start(bf16[2,128,1024]{2,1,0:T(8,128)(2,1)} %grad_hbm.1) | copy-start | bytes 1572868
  5.5 1.0 %copy-start.4 = (bf16[1,2,192,640]{3,2,1,0:T(8,128)(2,1)S(1)}, bf16[1,2,192,640]{3,2,1,0:T(8,128)(2,1)}, u32[]{:S(2)}) copy-start(bf16[1,2,192,640]{3,2,1,0:T(8,128)(2,1)} %param.16) | copy-start | bytes 1474564
  6.5 0.8 %copy-start.5 = (bf16[1,32,1024]{2,1,0:T(8,128)(2,1)S(1)}, bf16[1,32,1024]{2,1,0:T(8,128)(2,1)}, u32[]{:S(2)}) copy-start(bf16[1,32,1024]{2,1,0:T(8,128)(2,1)} %param.17) | copy-start | bytes 196612
  7.3 0.8 %copy-start.6 = (bf16[1,32,1024]{2,1,0:T(8,128)(2,1)S(1)}, bf16[1,32,1024]{2,1,0:T(8,128)(2,1)}, u32[]{:S(2)}) copy-start(bf16[1,32,1024]{2,1,0:T(8,128)(2,1)} %param.19) | copy-start | bytes 196612
  8.2 0.7 %copy-start.7 = (bf16[1,1024]{1,0:T(2,128)(2,1)S(1)}, bf16[1,1024]{1,0:T(2,128)(2,1)}, u32[]{:S(2)}) copy-start(bf16[1,1024]{1,0:T(2,128)(2,1)} %gain_ref.1) | copy-start | bytes 6148
  8.9 0.7 %copy-start.8 = (s32[1,2,128]{2,1,0:T(2,128)S(1)}, s32[1,2,128]{2,1,0:T(2,128)}, u32[]{:S(2)}) copy-start(s32[1,2,128]{2,1,0:T(2,128)} %param.14) | copy-start | bytes 3076
  9.5 0.7 %copy-start.9 = (s32[1,2,128]{2,1,0:T(2,128)S(1)}, s32[1,2,128]{2,1,0:T(2,128)}, u32[]{:S(2)}) copy-start(s32[1,2,128]{2,1,0:T(2,128)} %param.15) | copy-start | bytes 3076
